TPU v7x, 32 devices: a whole 2x2x4 slice. The times are simulated.
32 devices in a mesh: fsdp: 8 (over y, x, core), rep: 4 (over z).
Axes of the slice: x: 2, y: 2, z: 4, core: 2. Of those that a mesh axis runs over, the one named last changes fastest.
Arguments:
- tokens: bfloat16 [16384, 1024], P(('fsdp', 'rep')), may hold values from -6 to 6
- lengths: int32 [64], P(('fsdp', 'rep')), may hold values from 64 to 256, as said below
- cotangent: float32 [16384, 1024], P(('fsdp', 'rep')), may hold values from -6 to 6
- qkv_weight: bfloat16 [1024, 3072], P('fsdp'), may hold values from -0.1875 to 0.1875
- out_weight: bfloat16 [1024, 1024], P('fsdp'), may hold values from -0.75 to 0.75
- up_weight: bfloat16 [1024, 4096], P('fsdp'), may hold values from -0.1875 to 0.1875
- down_weight: bfloat16 [4096, 1024], P('fsdp'), may hold values from -0.09375 to 0.09375
- biases: bfloat16 [6, 1024], P(None, 'fsdp'), may hold values from -3 to 3
- up_bias: bfloat16 [4096], P('fsdp'), may hold values from -3 to 3
- gains: bfloat16 [2, 1024], P(None, 'fsdp'), may hold values from 0.5 to 1.5
Outputs:
- layer_out: bfloat16 [16384, 1024], P(('fsdp', 'rep'))
- token_grad: float32 [16384, 1024], P(('fsdp', 'rep'))
- qkv_grad: float32 [1024, 3072], P('fsdp')
- out_grad: float32 [1024, 1024], P('fsdp')
- up_grad: float32 [1024, 4096], P('fsdp')
- down_grad: float32 [4096, 1024], P('fsdp')
- biases_grad: float32 [6, 1024], P(None, 'fsdp')
- up_bias_grad: float32 [4096], P('fsdp')
- gains_grad: float32 [2, 1024], P(None, 'fsdp')
Inputs may be any that keep to these rules, and one draw needn't show every extreme that they name: lengths[s] is the number of live positions of sequence slot s; in every draw some slot holds 256 live positions and some holds 64.
All inputs are finite; a program needn't handle non-finite values.
Results may differ from a plain program's by a relative error of at most 0.017.
Values may be sent and summed in bfloat16 or wider, within the bound.
A program may use at most 192 MiB of HBM per device.

v0:
```python
import math

import jax
import jax.numpy as jnp
from jax import lax
from jax.experimental import pallas as pl
from jax.experimental.pallas import tpu as pltpu
from jax.sharding import PartitionSpec as P

HEAD_SIZE = 64


def matmul(left_side, right_side):
    return jnp.dot(left_side, right_side, preferred_element_type=jnp.float32)


def transposed_left(left_side, right_side):
    return lax.dot_general(
        left_side, right_side, (((0,), (0,)), ((), ())), preferred_element_type=jnp.float32
    )


def transposed_right(left_side, right_side):
    return lax.dot_general(
        left_side, right_side, (((1,), (1,)), ((), ())), preferred_element_type=jnp.float32
    )


def column_sum(values):
    return jnp.sum(values.astype(jnp.float32), axis=0)


def row_mean(values):
    return jnp.mean(values, axis=-1, keepdims=True)


def normalize(hidden):
    center = hidden - row_mean(hidden)
    inverse = lax.rsqrt(row_mean(center * center) + 1e-05)
    return center * inverse, inverse


def norm_back(grad, norm, inverse, gain):
    scaled = grad * gain
    return inverse * (scaled - row_mean(scaled) - norm * row_mean(scaled * norm))


def low(values):
    return values.astype(jnp.bfloat16)


def gather_small(biases, up_bias, gains):
    width, up_width = biases.shape[1], up_bias.shape[0]
    packed = jnp.concatenate([biases.reshape(-1), gains.reshape(-1), up_bias])
    everyone = lax.all_gather(packed, "fsdp", axis=0, tiled=False).astype(jnp.float32)
    rows = everyone[:, : 8 * width].reshape(-1, 8, width).transpose(1, 0, 2).reshape(8, -1)
    return rows[:6], everyone[:, 8 * width : 8 * width + up_width].reshape(-1), rows[6:]


def reduce_weight(grad):
    shard = lax.psum_scatter(low(grad), "fsdp", scatter_dimension=0, tiled=True)
    return lax.psum(shard, "rep").astype(jnp.float32)


def portable(
    tokens,
    lengths,
    cotangent,
    qkv_weight,
    out_weight,
    up_weight,
    down_weight,
    biases,
    up_bias,
    gains,
):
    slots = lengths.shape[0]
    rows, width = tokens.shape
    seq = rows // slots
    heads = width // HEAD_SIZE
    scale = 1.0 / math.sqrt(HEAD_SIZE)
    w_qkv = lax.all_gather(qkv_weight, "fsdp", axis=0, tiled=True)
    w_out = lax.all_gather(out_weight, "fsdp", axis=0, tiled=True)
    w_up = lax.all_gather(up_weight, "fsdp", axis=0, tiled=True)
    w_down = lax.all_gather(down_weight, "fsdp", axis=0, tiled=True)
    bias_rows, bias_up, gain_rows = gather_small(biases, up_bias, gains)

    def split(values):
        return values.reshape(slots, seq, heads, HEAD_SIZE)

    def join(values):
        return values.reshape(rows, width)

    sums = matmul(tokens, w_qkv)
    query = split(low(sums[:, :width] + bias_rows[0]))
    key = split(low(sums[:, width : 2 * width]))
    value = split(low(sums[:, 2 * width :] + bias_rows[1]))
    live = jnp.arange(seq)[None, :] < lengths[:, None]
    scores = scale * jnp.einsum(
        "bshd,bthd->bhst", query, key, preferred_element_type=jnp.float32
    )
    scores = jnp.where(live[:, None, None, :], scores, -1e30)
    exps = jnp.exp(scores - jnp.max(scores, axis=-1, keepdims=True))
    probs = exps / jnp.sum(exps, axis=-1, keepdims=True)
    probs_low = low(probs)
    mixed = low(
        join(jnp.einsum("bhst,bthd->bshd", probs_low, value, preferred_element_type=jnp.float32))
    )
    first, first_inverse = normalize(
        tokens.astype(jnp.float32) + matmul(mixed, w_out) + bias_rows[2]
    )
    first_norm = first * gain_rows[0] + bias_rows[3]
    first_low = low(first_norm)
    inner = matmul(first_low, w_up) + bias_up
    cumulative = 0.5 * (1.0 + lax.erf(inner * math.sqrt(0.5)))
    act_low = low(inner * cumulative)
    slope = low(cumulative + inner * jnp.exp(-0.5 * inner * inner) / math.sqrt(2.0 * math.pi))
    second, second_inverse = normalize(first_norm + matmul(act_low, w_down) + bias_rows[4])
    layer_out = low(second * gain_rows[1] + bias_rows[5])

    grad_out = cotangent * live.reshape(rows, 1).astype(jnp.float32)
    grad_h2 = norm_back(grad_out, second, second_inverse, gain_rows[1])
    grad_branch = low(grad_h2)
    down_grad = reduce_weight(transposed_left(act_low, grad_branch))
    grad_inner = low(transposed_right(grad_branch, w_down) * slope)
    up_grad = reduce_weight(transposed_left(first_low, grad_inner))
    grad_first = grad_h2 + transposed_right(grad_inner, w_up)
    grad_h1 = norm_back(grad_first, first, first_inverse, gain_rows[0])
    grad_attn = low(grad_h1)
    out_grad = reduce_weight(transposed_left(mixed, grad_attn))
    grad_mixed = split(low(transposed_right(grad_attn, w_out)))
    grad_probs = jnp.einsum(
        "bshd,bthd->bhst", grad_mixed, value, preferred_element_type=jnp.float32
    )
    shared = jnp.sum(probs * grad_probs, axis=-1, keepdims=True)
    grad_scores = low(probs * (grad_probs - shared))
    grad_query = scale * jnp.einsum(
        "bhst,bthd->bshd", grad_scores, key, preferred_element_type=jnp.float32
    )
    grad_key = scale * jnp.einsum(
        "bhst,bshd->bthd", grad_scores, query, preferred_element_type=jnp.float32
    )
    grad_value = jnp.einsum(
        "bhst,bshd->bthd", probs_low, grad_mixed, preferred_element_type=jnp.float32
    )
    grad_qkv = jnp.concatenate(
        [join(low(grad_query)), join(low(grad_key)), join(low(grad_value))], axis=1
    )
    qkv_grad = reduce_weight(transposed_left(tokens, grad_qkv))
    token_grad = grad_h1 + transposed_right(grad_qkv, w_qkv)
    small = jnp.stack(
        [
            column_sum(grad_qkv[:, :width]),
            column_sum(grad_qkv[:, 2 * width :]),
            column_sum(grad_attn),
            column_sum(grad_first),
            column_sum(grad_branch),
            column_sum(grad_out),
            column_sum(grad_first * first),
            column_sum(grad_out * second),
        ]
    )
    owner = lax.axis_index("fsdp")
    small, up_sum = lax.psum((small, column_sum(grad_inner)), ("fsdp", "rep"))
    own, own_up = biases.shape[1], up_bias.shape[0]
    small = lax.dynamic_slice(small, (0, owner * own), (8, own))
    up_bias_grad = lax.dynamic_slice(up_sum, (owner * own_up,), (own_up,))
    return (
        layer_out,
        token_grad,
        qkv_grad,
        out_grad,
        up_grad,
        down_grad,
        small[:6],
        up_bias_grad,
        small[6:],
    )


MESH = pl.DeviceIdType.MESH
F32 = jnp.float32
BF16 = jnp.bfloat16
MIB = 1 << 20


def dot_nn(a, b):
    return lax.dot_general(a, b, (((1,), (0,)), ((), ())), preferred_element_type=F32)


def dot_nt(a, b):
    return lax.dot_general(a, b, (((1,), (1,)), ((), ())), preferred_element_type=F32)


def dot_tn(a, b):
    return lax.dot_general(a, b, (((0,), (0,)), ((), ())), preferred_element_type=F32)


class Place:
    def __init__(self):
        f, z = lax.axis_index("fsdp"), lax.axis_index("rep")
        self.f, self.z = f, z
        self.core = lax.rem(f, 2)
        self.x = lax.rem(lax.div(f, 2), 2)
        self.y = lax.div(f, 4)
        self.chip = lax.div(f, 2)
        self.fx = f + 2 - 4 * self.x
        self.fy = f + 4 - 8 * self.y
        self.fd = self.fx + 4 - 8 * self.y
        self.fs = f + 1 - 2 * self.core
        self.par = lax.rem(z, 2)
        self.zn = z + 1 - 2 * self.par

    def dev(self, f=None, z=None):
        return {"fsdp": self.f if f is None else f, "rep": self.z if z is None else z}


def remote(src, dst, send_sem, recv_sem, device):
    return pltpu.make_async_remote_copy(
        src_ref=src, dst_ref=dst, send_sem=send_sem, recv_sem=recv_sem,
        device_id=device, device_id_type=MESH,
    )


UNITS = (
    ("q", 0, 32, 0),
    ("q", 32, 32, 0),
    ("q", 64, 32, 0),
    ("q", 96, 32, 0),
    ("o", 0, 128, 0),
    ("u", 0, 64, 0),
    ("u", 64, 64, 0),
    ("d", 0, 128, 0),
    ("d", 128, 128, 0),
    ("d", 256, 128, 16),
    ("d", 384, 128, 16),
)
FORWARD_PLAN = (
    ("direct", 0), ("direct", 1), ("direct", 2), ("direct", 3), ("small", 0), ("fx", 0), ("fy", 0),
    ("direct", 4), ("fx", 1), ("fy", 1), ("fx", 2), ("fy", 2), ("r2", 0), ("fx", 3), ("fy", 3), ("r3", 0),
    ("r5", 0), ("r4", 0), ("r2", 1), ("r3", 1), ("direct", 5), ("fx", 4), ("fy", 4), ("r2", 2), ("r5", 1),
    ("r4", 1), ("r3", 2), ("r5", 2), ("r4", 2), ("r2", 3), ("r5", 3), ("r4", 3), ("r3", 3), ("direct", 6),
    ("done", 0), ("done", 1), ("done", 2), ("done", 3), ("qkv", 0), ("fx", 5), ("fy", 5), ("r2", 4),
    ("r3", 4), ("at", 0, 1), ("r4", 4), ("r5", 4), ("at", 1, 4), ("direct", 7), ("at", 4, 6), ("fx", 6),
    ("fy", 6), ("at", 6, 8), ("r2", 5), ("at", 8, 12), ("r4", 5), ("r5", 5), ("direct", 8), ("at", 12, 13),
    ("r3", 5), ("at", 13, 14), ("fx", 7), ("fy", 7), ("at", 14, 16), ("done", 4), ("out", 0), ("r2", 6),
    ("r4", 6), ("r5", 6), ("direct", 9), ("fx", 8), ("fy", 8), ("r3", 6), ("direct", 10), ("r5", 7),
    ("r4", 7), ("done", 5), ("done", 6), ("up", 0, 1), ("r2", 7), ("up", 1, 2), ("fx", 9), ("fy", 9),
    ("up", 2, 3), ("r3", 7), ("up", 3, 4), ("r4", 8), ("r5", 8), ("up", 4, 5), ("r2", 8), ("up", 5, 7),
    ("fx", 10), ("fy", 10), ("r3", 8), ("up", 7, 8), ("r2", 9), ("r4", 9), ("r5", 9), ("done", 7), ("dn", 7),
    ("r3", 9), ("done", 8), ("dn", 8), ("r2", 10), ("r4", 10), ("r5", 10), ("done", 9), ("tidy", 0),
    ("dn", 9), ("r3", 10), ("done", 10), ("dn", 10), ("last", 0),
)
KINDS = 13


class Gather:
    def __init__(self, place, unit, shard, full, base, rows, extra, send, recv, local):
        self.p, self.unit, self.shard, self.full = place, unit, shard, full
        self.base, self.rows, self.size = base, rows, shard.shape[0]
        self.send_sem, self.recv_sem, self.local_sem = send, recv, local
        p, half = place, rows // 2
        one, two = half * p.par, half * (1 - p.par)
        wide, rest = half + extra, half - extra
        near_x, near_y = rest * p.par, rest * (1 - p.par)
        far_x, far_y = wide * (1 - p.par), wide * p.par
        to_x, to_y, to_s, to_z = p.dev(f=p.fx), p.dev(f=p.fy), p.dev(f=p.fs), p.dev(z=p.zn)
        sx, sy, sd = (g + 1 - 2 * p.core for g in (p.fx, p.fy, p.fd))
        self.table = (
            ((p.fx, near_x), (p.f, near_x), wide, to_x),
            ((p.fy, near_y), (p.f, near_y), wide, to_y),
            ((p.fx, far_x), (p.fx, far_y), rest, to_z),
            ((p.fy, far_y), (p.fy, far_x), rest, to_z),
            ((p.fd, one), (p.fx, one), half, to_y),
            ((p.fd, two), (p.fy, two), half, to_x),
            ((p.fs, 0), (p.f, 0), rows, to_s),
            ((sx, near_x), (p.fx, near_x), wide, to_s),
            ((sy, near_y), (p.fy, near_y), wide, to_s),
            ((sx, far_x), (p.fx, far_x), rest, to_s),
            ((sy, far_y), (p.fy, far_y), rest, to_s),
            ((sd, one), (p.fd, one), half, to_s),
            ((sd, two), (p.fd, two), half, to_s),
        )

    def at(self, owner, lo, n):
        return self.full.at[pl.ds(pl.multiple_of(owner * self.size + self.base + lo, 16), n)]

    def copy(self, kind, sending):
        received, sent, n, device = self.table[kind]
        owner, lo = sent if sending else received
        here = self.at(owner, lo, n)
        src = self.shard.at[pl.ds(pl.multiple_of(self.base + lo, 16), n)] if kind in (0, 1, 6) else here
        return remote(src, here, self.send_sem.at[self.unit, kind], self.recv_sem.at[self.unit, kind], device)

    def start(self, *kinds):
        for kind in kinds:
            self.copy(kind, True).start()

    def got(self, *kinds):
        for kind in kinds:
            self.copy(kind, False).wait_recv()

    def sent(self):
        for kind in range(KINDS):
            self.copy(kind, True).wait_send()

    def own(self):
        src = self.shard.at[pl.ds(self.base, self.rows)]
        return pltpu.make_async_copy(src, self.at(self.p.f, 0, self.rows), self.local_sem.at[self.unit])

    def direct(self):
        self.start(0, 1, 6)
        self.own().start()

    def pass_on(self, arrived, *kinds):
        self.got(arrived)
        self.start(*kinds)

    def done(self):
        self.got(6, 7, 8, 9, 10, 11, 12)
        self.own().wait()


def forward_kernel(
    lengths, tokens, cot, small, sh_q, sh_o, sh_u, sh_d,
    layer_out, wq_out, wo_out, wu_out, wd_out, qkv_out, slope_out, act_pair, first_pair, mixed_pair,
    tok_pair, branch_pair, norm_out, inv_out, grad_out_ref, params_out, sums_out,
    x, wq, wo, wu, wd, qkv, mixed, norm, first_low, act, slope, acc, cot_v, gh2, out_v, gb, smalls, params,
    inv_v, sums, up_rows,
    ag_send, ag_recv, ag_local, sm_send, sm_recv, sm_local, io, pair_send, pair_recv, pair_local, wd_sem,
):
    p = Place()
    rows, width = x.shape
    slots = lengths.shape[0]
    seq = rows // slots
    others = [lax.rem(p.f + k, 8) for k in range(1, 8)]
    barrier = pltpu.get_barrier_semaphore()
    for g in others:
        pl.semaphore_signal(barrier, inc=1, device_id=p.dev(f=g), device_id_type=MESH)
    pl.semaphore_signal(barrier, inc=1, device_id=p.dev(z=p.zn), device_id_type=MESH)
    loads = [
        pltpu.make_async_copy(tokens, x, io.at[0]),
        pltpu.make_async_copy(cot, cot_v, io.at[1]),
        pltpu.make_async_copy(small, smalls.at[p.f], sm_local),
    ]
    for c in loads:
        c.start()
    pl.semaphore_wait(barrier, 8)

    def small_copy(k, owner, device):
        return remote(small, smalls.at[owner], sm_send.at[k], sm_recv.at[k], device)

    for k, g in enumerate(others):
        small_copy(k, p.f, p.dev(f=g)).start()

    weights = {"q": (sh_q, wq), "o": (sh_o, wo), "u": (sh_u, wu), "d": (sh_d, wd)}
    parts = [Gather(p, i, *weights[n], *piece, ag_send, ag_recv, ag_local) for i, (n, *piece) in enumerate(UNITS)]

    mine = pl.ds(pl.multiple_of(p.core * rows, rows), rows)

    def pair(index, chip, src, dst, cols):
        own = pl.ds(pl.multiple_of((2 * chip + p.core) * cols, cols), cols)
        other = pl.ds(pl.multiple_of((2 * chip + 1 - p.core) * cols, cols), cols)
        here = dst.at[mine, pl.ds(chip * cols, cols)]
        return (
            pltpu.make_async_copy(src.at[:, own], here, pair_local.at[index, chip]),
            remote(src.at[:, other], here, pair_send.at[index, chip], pair_recv.at[index, chip], p.dev(f=p.fs)),
        )

    pairs = []

    def start_pair(index, src, dst, cols, chips=range(4)):
        for chip in chips:
            for c in pair(index, chip, src, dst, cols):
                c.start()
            pairs.append((index, chip, src, dst, cols))

    stores = []

    def store(src, dst, sem):
        stores.append(pltpu.make_async_copy(src, dst, sem))
        stores[-1].start()

    def small_params(_):
        loads[0].wait()
        start_pair(0, x, tok_pair, 128)
        loads[2].wait()
        for k in range(7):
            back = lax.rem(p.f + 7 - k, 8)
            small_copy(k, back, p.dev(f=back)).wait_recv()
        for g in range(8):
            part = smalls[g].astype(F32)
            params[:, g * 128 : (g + 1) * 128] = part
            for j in range(4):
                up_rows[g : g + 1, j * 128 : (j + 1) * 128] = part[8 + j : 9 + j]

    def project(_):
        store(wq, wq_out, io.at[2])
        for j in range(3):
            part = dot_nn(x[...], wq[:, j * width : (j + 1) * width])
            if j == 0:
                part = part + params[0:1]
            if j == 2:
                part = part + params[1:2]
            qkv[:, j * width : (j + 1) * width] = part.astype(BF16)
        store(qkv, qkv_out, io.at[3])

    left = lax.broadcasted_iota(jnp.int32, (seq, 128), 1) < HEAD_SIZE
    key_row = lax.broadcasted_iota(jnp.int32, (seq, seq), 0)

    def attend(step, carry):
        slot, pair_of = lax.div(step, 8), lax.rem(step, 8)
        at_rows = pl.ds(pl.multiple_of(slot * seq, seq), seq)
        col = pl.multiple_of(pair_of * 128, 128)
        q = qkv[at_rows, pl.ds(col, 128)]
        k = qkv[at_rows, pl.ds(pl.multiple_of(width + col, 128), 128)]
        v = qkv[at_rows, pl.ds(pl.multiple_of(2 * width + col, 128), 128)]
        dead = key_row >= lengths[slot]
        outs = []
        for head in range(2):
            k_head = jnp.where(left if head == 0 else ~left, k, jnp.zeros_like(k))
            scores = dot_nt(k_head, q) * (1.0 / math.sqrt(HEAD_SIZE))
            scores = jnp.where(dead, -1e30, scores)
            exps = jnp.exp(scores - jnp.max(scores, axis=0, keepdims=True))
            probs = exps * (1.0 / jnp.sum(exps, axis=0, keepdims=True))
            outs.append(dot_tn(probs.astype(BF16), v))
        mixed[at_rows, pl.ds(col, 128)] = jnp.where(left, outs[0], outs[1]).astype(BF16)
        return carry

    steps = 8 * slots

    def attention(first, last):
        lax.fori_loop(first * steps // 16, last * steps // 16, attend, 0)
        if last == 16:
            start_pair(1, mixed, mixed_pair, 128)

    def first_norm(_):
        store(wo, wo_out, io.at[4])
        hidden = x[...].astype(F32) + dot_nn(mixed[...], wo[...]) + params[2:3]
        center = hidden - row_mean(hidden)
        inverse = lax.rsqrt(row_mean(center * center) + 1e-05)
        norm[...] = center * inverse
        inv_v[...] = jnp.broadcast_to(inverse, inv_v.shape)
        shifted = norm[...] * params[6:7] + params[3:4]
        first_low[...] = shifted.astype(BF16)
        acc[...] = shifted + params[4:5]
        start_pair(2, first_low, first_pair, 128)
        store(norm, norm_out, io.at[5])
        store(inv_v, inv_out, io.at[6])

    def up_step(j, carry):
        cols = pl.ds(pl.multiple_of(j * 512, 512), 512)
        inner = dot_nn(first_low[...], wu[:, cols]) + up_rows[pl.ds(j, 1), :]
        phi = 0.5 * (1.0 + lax.erf(inner * math.sqrt(0.5)))
        act[:, cols] = (inner * phi).astype(BF16)
        density = jnp.exp(-0.5 * inner * inner) * (1.0 / math.sqrt(2.0 * math.pi))
        slope[:, cols] = (phi + inner * density).astype(BF16)
        return carry

    def up(first, last):
        if first == 0:
            store(wu, wu_out, io.at[7])
        lax.fori_loop(first, last, up_step, 0)
        if last == 4:
            start_pair(3, act, act_pair, 512, range(2))
        if last == 8:
            start_pair(3, act, act_pair, 512, range(2, 4))
            store(slope, slope_out, io.at[8])

    def down(u):
        _, lo, n, _ = UNITS[u]
        for g in range(8):
            at = pl.ds(g * 512 + lo, n)
            store(wd.at[at], wd_out.at[at], wd_sem.at[g, u])
        for j in range(0, 8, 1024 // n):
            cols = [slice(512 * g + lo, 512 * g + lo + n) for g in range(j, j + 1024 // n)]
            left = jnp.concatenate([act[:, c] for c in cols], axis=1)
            right = jnp.concatenate([wd[c, :] for c in cols], axis=0)
            acc[...] += dot_nn(left, right)

    tidied = []

    def tidy(_):
        for k, g in enumerate(others):
            small_copy(k, p.f, p.dev(f=g)).wait_send()
        for part in parts:
            if UNITS[part.unit][0] != "d":
                part.sent()
        count = len(stores) - 8
        for c in stores[:count]:
            c.wait()
        for args in pairs[:12]:
            for c in pair(*args):
                c.wait()
        tidied.append(count)

    def second_norm(_):
        loads[1].wait()
        hidden = acc[...]
        center = hidden - row_mean(hidden)
        inverse = lax.rsqrt(row_mean(center * center) + 1e-05)
        second = center * inverse
        row_at = lax.broadcasted_iota(jnp.int32, (seq, 1), 0)
        live = jnp.concatenate([(row_at < lengths[s]).astype(F32) for s in range(slots)], axis=0)
        e = cot_v[...] * live
        scaled = e * params[7:8]
        gh2[...] = inverse * (scaled - row_mean(scaled) - second * row_mean(scaled * second))
        gb[...] = gh2[...].astype(BF16)
        swap = (
            pltpu.make_async_copy(gb, branch_pair.at[mine], pair_local.at[4, 0]),
            remote(gb, branch_pair.at[mine], pair_send.at[4, 0], pair_recv.at[4, 0], p.dev(f=p.fs)),
        )
        for c in swap:
            c.start()
        store(gh2, grad_out_ref, io.at[11])
        store(params, params_out, io.at[12])
        out_v[...] = (second * params[7:8] + params[5:6]).astype(BF16)
        store(out_v, layer_out, io.at[10])
        sums[...] = jnp.zeros_like(sums)
        sums[0:1] = jnp.sum(e * second, axis=0, keepdims=True)
        sums[1:2] = jnp.sum(e, axis=0, keepdims=True)
        sums[2:3] = jnp.sum(gb[...].astype(F32), axis=0, keepdims=True)
        store(sums, sums_out, io.at[13])
        for part in parts:
            if UNITS[part.unit][0] == "d":
                part.sent()
        for args in pairs[12:]:
            for c in pair(*args):
                c.wait()
        for c in stores[tidied[0] :]:
            c.wait()
        for c in swap:
            c.wait()

    work = {
        "small": small_params, "qkv": project, "at": attention, "out": first_norm, "up": up, "dn": down,
        "tidy": tidy, "last": second_norm,
        "direct": lambda u: parts[u].direct(), "done": lambda u: parts[u].done(),
        "fx": lambda u: parts[u].pass_on(0, 4, 2, 7), "fy": lambda u: parts[u].pass_on(1, 5, 3, 8),
        "r2": lambda u: parts[u].pass_on(2, 9), "r3": lambda u: parts[u].pass_on(3, 10),
        "r4": lambda u: parts[u].pass_on(4, 11), "r5": lambda u: parts[u].pass_on(5, 12),
    }
    for name, *which in FORWARD_PLAN:
        work[name](*which)


def forward_call(tokens, lengths, cotangent, qkv_w, out_w, up_w, down_w, small):
    rows, width = tokens.shape
    ff = up_w.shape[1]
    anyspace = pl.BlockSpec(memory_space=pl.ANY)
    shape = jax.ShapeDtypeStruct
    outs = [
        shape((rows, width), BF16),
        shape((width, 3 * width), BF16),
        shape((width, width), BF16),
        shape((width, ff), BF16),
        shape((ff, width), BF16),
        shape((rows, 3 * width), BF16),
        shape((rows, ff), BF16),
        shape((2 * rows, ff // 2), BF16),
        shape((2 * rows, width // 2), BF16),
        shape((2 * rows, width // 2), BF16),
        shape((2 * rows, width // 2), BF16),
        shape((2 * rows, width), BF16),
        shape((rows, width), F32),
        shape((rows, 128), F32),
        shape((rows, width), F32),
        shape((16, width), F32),
        shape((8, width), F32),
    ]
    dma = pltpu.SemaphoreType.DMA
    scratch = [
        pltpu.VMEM((rows, width), BF16),
        pltpu.VMEM((width, 3 * width), BF16),
        pltpu.VMEM((width, width), BF16),
        pltpu.VMEM((width, ff), BF16),
        pltpu.VMEM((ff, width), BF16),
        pltpu.VMEM((rows, 3 * width), BF16),
        pltpu.VMEM((rows, width), BF16),
        pltpu.VMEM((rows, width), F32),
        pltpu.VMEM((rows, width), BF16),
        pltpu.VMEM((rows, ff), BF16),
        pltpu.VMEM((rows, ff), BF16),
        pltpu.VMEM((rows, width), F32),
        pltpu.VMEM((rows, width), F32),
        pltpu.VMEM((rows, width), F32),
        pltpu.VMEM((rows, width), BF16),
        pltpu.VMEM((rows, width), BF16),
        pltpu.VMEM((8, 16, 128), BF16),
        pltpu.VMEM((16, width), F32),
        pltpu.VMEM((rows, 128), F32),
        pltpu.VMEM((8, width), F32),
        pltpu.VMEM((8, ff // 8), F32),
        dma((len(UNITS), KINDS)),
        dma((len(UNITS), KINDS)),
        dma((len(UNITS),)),
        dma((7,)),
        dma((7,)),
        dma,
        dma((14,)),
        dma((5, 4)),
        dma((5, 4)),
        dma((5, 4)),
        dma((8, len(UNITS))),
    ]
    return pl.pallas_call(
        forward_kernel,
        out_shape=outs,
        in_specs=[pl.BlockSpec(memory_space=pltpu.SMEM)] + [anyspace] * 7,
        out_specs=[anyspace] * len(outs),
        scratch_shapes=scratch,
        name="forward",
        cost_estimate=pl.CostEstimate(flops=2 * 512 * 12582912, bytes_accessed=60 * MIB, transcendentals=4 * MIB),
        compiler_params=pltpu.CompilerParams(
            collective_id=0, has_side_effects=True, vmem_limit_bytes=60 * MIB
        ),
    )(lengths, tokens, cotangent, small, qkv_w, out_w, up_w, down_w)


def pack_small(biases, up_bias, gains):
    return jnp.concatenate([biases, gains, up_bias.reshape(4, 128), jnp.zeros((4, 128), BF16)], axis=0)


BLOCKS = 12
SHARED = (2, 3)
PIECES = (
    (0, 0, 64),
    (1, 0, 64),
    (2, None, 32),
    (4, 0, 64),
    (3, None, 32),
    (5, 0, 64),
    (6, 0, 64),
    (7, 0, 64),
    (8, 0, 64),
    (9, 0, 32),
    (9, 32, 32),
    (10, 0, 32),
    (10, 32, 32),
    (11, 0, 16),
    (11, 16, 16),
    (11, 32, 16),
    (11, 48, 16),
)
PLAN = (
    ("start", 0), ("down", 0), ("begin", 0), ("down", 1), ("begin", 1), ("down", 2), ("down", 3), ("g", 0),
    ("h", 0), ("second", 0), ("g", 1), ("h", 1), ("u", 0), ("second", 1), ("begin", 3), ("g", 2),
    ("along", 0), ("h", 2), ("u", 1), ("along", 1), ("begin", 2), ("g", 3), ("begin", 5), ("h", 3), ("u", 2),
    ("second", 3), ("norm", 0), ("second", 2), ("u", 3), ("inward", 0), ("begin", 4), ("gm", 0),
    ("second", 5), ("o", 0), ("at", 0, 1), ("hand", 0), ("inward", 1), ("along", 3), ("at", 1, 2),
    ("along", 2), ("begin", 6), ("at", 2, 4), ("second", 4), ("at", 4, 5), ("pass", 0), ("inward", 3),
    ("at", 5, 6), ("along", 5), ("at", 6, 7), ("hand", 1), ("begin", 7), ("inward", 2), ("at", 7, 8),
    ("at", 8, 9), ("hand", 3), ("at", 9, 10), ("inward", 5), ("pass", 1), ("second", 6), ("at", 10, 11),
    ("along", 4), ("at", 11, 12), ("hand", 2), ("at", 12, 13), ("inward", 4), ("begin", 8), ("at", 13, 14),
    ("pass", 3), ("at", 14, 15), ("second", 7), ("at", 15, 16), ("hand", 5), ("q", 0), ("along", 6), ("q", 1),
    ("close", 0), ("pass", 2), ("begin", 9), ("q", 2), ("hand", 4), ("inward", 6), ("small", 0),
    ("second", 8), ("pass", 5), ("t", 0), ("t", 1), ("pass", 4), ("along", 7), ("begin", 10), ("close", 1),
    ("t", 2), ("second", 9), ("hand", 6), ("level", 1), ("inward", 7), ("begin", 11), ("along", 8),
    ("begin", 12), ("second", 10), ("along", 9), ("close", 3), ("begin", 13), ("pass", 6), ("inward", 8),
    ("begin", 14), ("hand", 7), ("inward", 9), ("hand", 8), ("second", 11), ("close", 2), ("begin", 15),
    ("pass", 7), ("hand", 9), ("second", 12), ("along", 10), ("inward", 10), ("begin", 16), ("close", 5),
    ("second", 13), ("second", 14), ("along", 11), ("close", 4), ("second", 15), ("pass", 8), ("inward", 11),
    ("pass", 9), ("along", 12), ("second", 16), ("hand", 10), ("along", 13), ("inward", 12), ("along", 14),
    ("hand", 11), ("along", 15), ("along", 16), ("inward", 13), ("close", 6), ("pass", 10), ("inward", 14),
    ("hand", 12), ("inward", 15), ("pass", 11), ("inward", 16), ("hand", 13), ("hand", 14), ("close", 7),
    ("pass", 12), ("hand", 15), ("level", 2), ("hand", 16), ("pass", 13), ("pass", 14), ("pass", 15),
    ("pass", 16), ("close", 8), ("close", 9), ("close", 10), ("close", 11), ("close", 12), ("close", 13),
    ("close", 14), ("close", 15), ("close", 16),
)
S1X, S1Y, S2X, S2Y, Z1G, Z1K, Z2, FM, FE, FF = range(10)


class Reduce:
    def __init__(self, place, prod, got_x, got_y, end_x, end_y, from_end, from_mid, swapped, out_at, send, recv, local, swap_send, swap_recv):
        self.p = place
        self.prod, self.got_x, self.got_y, self.end_x, self.end_y = prod, got_x, got_y, end_x, end_y
        self.from_end, self.from_mid, self.swapped, self.out_at = from_end, from_mid, swapped, out_at
        self.send, self.recv, self.local = send, recv, local
        self.swap_send, self.swap_recv = swap_send, swap_recv
        z = place.z
        self.mid = 1 + lax.div(z, 2)
        self.end = 3 * lax.div(z, 2)
        self.is_mid = z == self.mid
        self.is_end = z == self.end

    def rows(self, u, theirs=False):
        b, o, n = PIECES[u]
        if o is None:
            o = pl.multiple_of(32 * (1 - self.p.par if theirs else self.p.par), 32)
        return b, o, n

    def z_rows(self, u):
        b, o, n = PIECES[u]
        return (b, 0, 64) if o is None else (b, o, n)

    def keep(self, o, n):
        return pl.ds(pl.multiple_of(64 * (self.mid - 1) + o, 16), n)

    def give(self, o, n):
        return pl.ds(pl.multiple_of(64 * (2 - self.mid) + o, 16), n)

    def copy(self, kind, u, sending=True):
        p = self.p
        b, o, n = self.rows(u, theirs=kind in (Z1G, Z1K) and not sending)
        _, oz, nz = self.z_rows(u)
        x, y, xn, yn = p.x, p.y, 1 - p.x, 1 - p.y
        near, far = pl.ds(o, n), pl.ds(64 + o, n)
        keep, give = self.keep(oz, nz), self.give(oz, nz)
        to_mid, to_end, to_other = p.dev(z=self.mid), p.dev(z=self.end), p.dev(z=3 - self.mid)
        own = self.prod.at[b, y, x]
        if kind == S1X:
            src, dst, dev = self.prod.at[b, :, xn, near], self.got_x.at[b, :, near], p.dev(f=p.fx)
        elif kind == S1Y:
            src, dst, dev = self.prod.at[b, yn, :, far], self.got_y.at[b, :, near], p.dev(f=p.fy)
        elif kind == S2Y:
            src, dst, dev = self.prod.at[b, yn, x, near], self.end_y.at[b, near], p.dev(f=p.fy)
        elif kind == S2X:
            src, dst, dev = self.prod.at[b, y, xn, far], self.end_x.at[b, near], p.dev(f=p.fx)
        elif kind == Z1G:
            src, dst, dev = own.at[self.give(o, n)], self.from_end.at[b, self.give(o, n)], to_mid
        elif kind == Z1K:
            src, dst, dev = own.at[self.keep(o, n)], self.from_end.at[b, self.keep(o, n)], to_mid
        elif kind == Z2:
            src, dst, dev = own.at[give], self.from_mid.at[b, pl.ds(oz, nz)], to_other
        elif kind == FM:
            src, dst, dev = own.at[keep], self.out_at(b, keep if sending else give), to_other
        elif kind == FE:
            src, dst, dev = own.at[keep], self.out_at(b, keep), to_end
        else:
            src, dst, dev = self.out_at(b, give), self.out_at(b, give), to_end
        return remote(src, dst, self.send.at[kind, u], self.recv.at[kind, u], dev)

    def swap(self, b, half):
        i = SHARED.index(b)
        src = self.prod.at[b, :, :, pl.ds(pl.multiple_of(64 * half + 32 * (1 - self.p.par), 32), 32)]
        dst = self.swapped.at[i, :, :, pl.ds(32 * half, 32)]
        return remote(src, dst, self.swap_send.at[i, half], self.swap_recv.at[i, half], self.p.dev(z=self.p.zn))

    def produced(self, b):
        if b in SHARED:
            self.swap(b, 0).start()
            self.swap(b, 1).start()

    def begin(self, u):
        b, o, n = self.rows(u)
        for half, kind in enumerate((S1X, S1Y)):
            if b in SHARED:
                at = pl.ds(pl.multiple_of(64 * half + o, 32), n)
                self.swap(b, half).wait()
                part = self.swapped[SHARED.index(b), :, :, 32 * half : 32 * half + 32]
                self.prod[b, :, :, at] = self.prod[b, :, :, at] + part
            self.copy(kind, u).start()

    def second(self, u):
        x, y = self.p.x, self.p.y
        b, o, n = self.rows(u)
        near, far = pl.ds(o, n), pl.ds(64 + o, n)
        self.copy(S1X, u).wait_recv()
        self.prod[b, :, x, near] = self.prod[b, :, x, near] + self.got_x[b, :, near]
        self.copy(S2Y, u).start()
        self.copy(S1Y, u).wait_recv()
        self.prod[b, y, :, far] = self.prod[b, y, :, far] + self.got_y[b, :, near]
        self.copy(S2X, u).start()

    def along(self, u):
        x, y = self.p.x, self.p.y
        b, o, n = self.rows(u)
        near, far = pl.ds(o, n), pl.ds(64 + o, n)
        self.copy(S2Y, u).wait_recv()
        self.prod[b, y, x, near] = self.prod[b, y, x, near] + self.end_y[b, near]
        self.copy(S2X, u).wait_recv()
        self.prod[b, y, x, far] = self.prod[b, y, x, far] + self.end_x[b, near]

        @pl.when(self.is_end)
        def _():
            self.copy(Z1G, u).start()
            self.copy(Z1K, u).start()

    def inward(self, u):
        x, y = self.p.x, self.p.y
        b, o, n = self.rows(u, theirs=True)

        @pl.when(self.is_mid)
        def _():
            give = self.give(o, n)
            self.copy(Z1G, u, False).wait_recv()
            if b in SHARED:
                self.prod[b, y, x, give] = self.from_end[b, give]
            else:
                self.prod[b, y, x, give] = self.prod[b, y, x, give] + self.from_end[b, give]
            self.copy(Z2, u).start()

    def write(self, u):
        b, o, n = self.z_rows(u)
        keep = self.keep(o, n)
        return pltpu.make_async_copy(
            self.prod.at[b, self.p.y, self.p.x, keep], self.out_at(b, keep), self.local.at[u]
        )

    def hand_out(self, u):
        x, y = self.p.x, self.p.y
        b, o, n = self.z_rows(u)

        @pl.when(self.is_mid)
        def _():
            keep = self.keep(o, n)
            self.copy(Z1K, u, False).wait_recv()
            if b in SHARED:
                part = self.keep(*self.rows(u, theirs=True)[1:])
                self.prod[b, y, x, part] = self.from_end[b, part]
            self.copy(Z2, u).wait_recv()
            total = self.prod[b, y, x, keep].astype(F32) + self.from_mid[b, o : o + n].astype(F32)
            if b not in SHARED:
                total = total + self.from_end[b, keep].astype(F32)
            self.prod[b, y, x, keep] = total.astype(BF16)
            self.copy(FM, u).start()
            self.copy(FE, u).start()
            self.write(u).start()

    def hand_on(self, u):
        @pl.when(self.is_mid)
        def _():
            self.copy(FM, u, False).wait_recv()
            self.copy(FF, u).start()

    def close(self, u):
        for kind in (S1X, S1Y, S2X, S2Y):
            self.copy(kind, u).wait_send()

        @pl.when(self.is_end)
        def _():
            self.copy(Z1G, u).wait_send()
            self.copy(Z1K, u).wait_send()
            self.copy(FE, u).wait_recv()
            self.copy(FF, u, False).wait_recv()

        @pl.when(self.is_mid)
        def _():
            for kind in (Z2, FM, FE, FF):
                self.copy(kind, u).wait_send()
            self.write(u).wait()


def backward_kernel(
    lengths, wq, wo, wu, wd, qkv, slope, act_pair, first_pair, mixed_pair, tok_pair, branch_pair,
    norm_in, inv_in, gh2, params_in, sums_in,
    token_grad, out_q, out_o, out_u, out_d, small_out,
    lhs, wbuf, slope_v, branch, gi, gq, gm, gh, norm, inv, params, sums_v, upsum,
    prod, got_x, got_y, end_x, end_y, from_end, from_mid, swapped,
    s_send, s_got, s_total, s_all, s_out,
    rs_send, rs_recv, rs_local, pair_send, pair_recv, load_sem, lhs_sem, w_sem, slope_sem,
    sm_send, sm_recv, smz_send, smz_recv, store_sem, swap_send, swap_recv,
):
    p = Place()
    rows, width = gh.shape
    slots = lengths.shape[0]
    seq = rows // slots
    planes = [lax.rem(p.f + k, 8) for k in range(1, 8)]
    levels = [lax.rem(p.z + k, 4) for k in range(1, 4)]
    barrier = pltpu.get_barrier_semaphore()
    for g in planes:
        pl.semaphore_signal(barrier, inc=1, device_id=p.dev(f=g), device_id_type=MESH)
    for g in levels:
        pl.semaphore_signal(barrier, inc=1, device_id=p.dev(z=g), device_id_type=MESH)

    mine = pl.ds(pl.multiple_of(p.core * rows, rows), rows)

    def lhs_copies(i):
        if i < 4:
            return [
                pltpu.make_async_copy(
                    act_pair.at[:, pl.ds(chip * 512 + i * 128, 128)],
                    lhs.at[i % 2, :, pl.ds(chip * 128, 128)],
                    lhs_sem.at[i, chip],
                )
                for chip in range(4)
            ]
        src = (first_pair, mixed_pair, tok_pair)[i - 4]
        return [pltpu.make_async_copy(src, lhs.at[i % 2], lhs_sem.at[i, 0])]

    def w_copy(i):
        if i < 8:
            j = i // 2
            src = wu.at[:, pl.ds(j * 1024, 1024)] if i % 2 else wd.at[pl.ds(j * 1024, 1024)]
        elif i == 8:
            src = wo
        else:
            src = wq.at[:, pl.ds((i - 9) * 1024, 1024)]
        return pltpu.make_async_copy(src, wbuf.at[i % 2], w_sem.at[i])

    def slope_copy(j):
        return pltpu.make_async_copy(slope.at[:, pl.ds(j * 1024, 1024)], slope_v.at[j % 2], slope_sem.at[j])

    loads = [
        pltpu.make_async_copy(src, dst, load_sem.at[i])
        for i, (src, dst) in enumerate(
            (
                (branch_pair, branch), (gh2, gh), (qkv, gq.at[mine]), (norm_in, norm), (inv_in, inv),
                (params_in, params), (sums_in, sums_v),
            )
        )
    ]
    for c in lhs_copies(0):
        c.start()
    loads[0].start()
    for c in lhs_copies(1):
        c.start()
    w_copy(0).start()
    slope_copy(0).start()
    for c in loads[1:]:
        c.start()

    def out_at(b, at):
        if b < 4:
            return out_d.at[pl.ds(128 * b, 128)].at[at]
        if b < 8:
            return out_u.at[at, pl.ds((b - 4) * 1024, 1024)]
        if b == 8:
            return out_o.at[at]
        return out_q.at[at, pl.ds((b - 9) * 1024, 1024)]

    red = Reduce(
        p, prod, got_x, got_y, end_x, end_y, from_end, from_mid, swapped, out_at, rs_send, rs_recv, rs_local,
        swap_send, swap_recv,
    )

    def produce(b, left, right):
        prod[b] = dot_tn(left, right).astype(BF16).reshape(2, 2, 128, 1024)
        red.produced(b)

    def to_pair(index, ref, cols):
        here = ref.at[mine, cols]
        return remote(here, here, pair_send.at[index], pair_recv.at[index], p.dev(f=p.fs))

    def block_cols(j):
        return pl.ds(j * 1024, 1024)

    whole = pl.ds(0, 1024)
    ga = branch

    def start(_):
        pl.semaphore_wait(barrier, 10)
        loads[0].wait()

    def down(b):
        for c in lhs_copies(b):
            c.wait()
        produce(b, lhs[b % 2], branch[...])
        for c in lhs_copies(b + 2):
            c.start()
        if b == 3:
            loads[1].wait()

    def inner_step(j):
        w_copy(2 * j).wait()
        w_copy(2 * j + 1).start()
        slope_copy(j).wait()
        if j < 3:
            slope_copy(j + 1).start()
        inner = (dot_nt(branch[mine], wbuf[0]) * slope_v[j % 2].astype(F32)).astype(BF16)
        gi[mine, j * 1024 : (j + 1) * 1024] = inner
        to_pair(j, gi, block_cols(j)).start()
        upsum[j : j + 1] = jnp.sum(inner.astype(F32), axis=0, keepdims=True)

    def hidden_step(j):
        w_copy(2 * j + 1).wait()
        w_copy(2 * j + 2).start()
        gh[...] += dot_nt(gi[mine, j * 1024 : (j + 1) * 1024], wbuf[1])
        if j == 0:
            for c in lhs_copies(4):
                c.wait()

    def up_block(j):
        to_pair(j, gi, block_cols(j)).wait_recv()
        produce(4 + j, lhs[0], gi[:, j * 1024 : (j + 1) * 1024])
        if j == 3:
            for c in lhs_copies(6):
                c.start()

    def first_norm(_):
        for c in loads[2:]:
            c.wait()
        e = gh[...]
        scaled = e * params[6:7]
        n = norm[...]
        sums_v[3:4] = jnp.sum(e, axis=0, keepdims=True)
        sums_v[4:5] = jnp.sum(e * n, axis=0, keepdims=True)
        gh[...] = inv[:, 0:1] * (scaled - row_mean(scaled) - n * row_mean(scaled * n))
        ga[mine] = gh[...].astype(BF16)
        to_pair(4, ga, whole).start()
        sums_v[5:6] = jnp.sum(ga[mine].astype(F32), axis=0, keepdims=True)

    def grad_mixed(_):
        w_copy(8).wait()
        w_copy(9).start()
        gm[...] = dot_nt(ga[mine], wbuf[0]).astype(BF16)
        w_copy(10).start()

    def out_block(_):
        for c in lhs_copies(5):
            c.wait()
        to_pair(4, ga, whole).wait_recv()
        produce(8, lhs[1], ga[...])

    left = lax.broadcasted_iota(jnp.int32, (seq, 128), 1) < HEAD_SIZE
    key_row = lax.broadcasted_iota(jnp.int32, (seq, seq), 0)
    scale = 1.0 / math.sqrt(HEAD_SIZE)

    def attend(step, carry):
        slot, pair_of = lax.rem(step, slots), lax.div(step, slots)
        at_rows = pl.ds(pl.multiple_of(slot * seq, seq), seq)
        own_rows = pl.ds(pl.multiple_of(p.core * rows + slot * seq, seq), seq)
        col = pl.multiple_of(pair_of * 128, 128)
        at_q = pl.ds(col, 128)
        at_k = pl.ds(pl.multiple_of(width + col, 128), 128)
        at_v = pl.ds(pl.multiple_of(2 * width + col, 128), 128)
        q, k, v = gq[own_rows, at_q], gq[own_rows, at_k], gq[own_rows, at_v]
        do = gm[at_rows, at_q]
        dead = key_row >= lengths[slot]
        parts = []
        for head in range(2):
            lanes = left if head == 0 else ~left
            k_head = jnp.where(lanes, k, jnp.zeros_like(k))
            v_head = jnp.where(lanes, v, jnp.zeros_like(v))
            scores = jnp.where(dead, -1e30, dot_nt(k_head, q) * scale)
            exps = jnp.exp(scores - jnp.max(scores, axis=0, keepdims=True))
            probs = exps * (1.0 / jnp.sum(exps, axis=0, keepdims=True))
            d_probs = dot_nt(v_head, do)
            shared = jnp.sum(probs * d_probs, axis=0, keepdims=True)
            d_scores = (probs * (d_probs - shared)).astype(BF16)
            parts.append(
                (dot_tn(d_scores, k) * scale, dot_nn(d_scores, q) * scale, dot_nn(probs.astype(BF16), do))
            )
        for at, one, two in zip((at_q, at_k, at_v), *parts):
            gq[own_rows, at] = jnp.where(left, one, two).astype(BF16)
        return carry

    steps = 8 * slots

    def attention(first, last):
        lax.fori_loop(first * steps // 16, last * steps // 16, attend, 0)
        if last % 8 == 0:
            half = last // 8 - 1
            for j in range(3):
                to_pair(5 + 3 * half + j, gq, pl.ds(j * 1024 + 512 * half, 512)).start()

    def qkv_block(j):
        if j == 0:
            for c in lhs_copies(6):
                c.wait()
        for half in range(2):
            to_pair(5 + 3 * half + j, gq, pl.ds(j * 1024 + 512 * half, 512)).wait_recv()
        produce(9 + j, lhs[0], gq[:, j * 1024 : (j + 1) * 1024])

    order = (6, 7, 5, 3, 2, 1, 4, 0)

    def small_to(k):
        g = planes[k]
        return remote(s_send.at[g], s_got.at[p.f], sm_send.at[k], sm_recv.at[k], p.dev(f=g))

    def small_from(k):
        g = lax.rem(p.f + 7 - k, 8)
        return remote(s_send.at[g], s_got.at[g], sm_send.at[k], sm_recv.at[k], p.dev(f=g))

    def level_to(k):
        return remote(s_total, s_all.at[p.z], smz_send.at[k], smz_recv.at[k], p.dev(z=levels[k]))

    def level_from(k):
        g = lax.rem(p.z + 3 - k, 4)
        return remote(s_total, s_all.at[g], smz_send.at[k], smz_recv.at[k], p.dev(z=g))

    stores = (
        pltpu.make_async_copy(gh, token_grad, store_sem.at[0]),
        pltpu.make_async_copy(s_out, small_out, store_sem.at[1]),
    )

    def small(_):
        sums_v[6:7] = jnp.sum(gq[mine, 0:1024].astype(F32), axis=0, keepdims=True)
        sums_v[7:8] = jnp.sum(gq[mine, 2048:3072].astype(F32), axis=0, keepdims=True)
        for g in range(8):
            cols = slice(g * 128, (g + 1) * 128)
            for i, row in enumerate(order):
                s_send[g, i : i + 1] = sums_v[row : row + 1, cols]
            for i in range(4):
                lo = (g % 2) * 512 + i * 128
                s_send[g, 8 + i : 9 + i] = upsum[g // 2 : g // 2 + 1, lo : lo + 128]
        for k in range(7):
            small_to(k).start()
        s_got[p.f] = s_send[p.f]

    def token_step(j):
        w_copy(9 + j).wait()
        gh[...] += dot_nt(gq[mine, j * 1024 : (j + 1) * 1024], wbuf[(9 + j) % 2])
        if j == 0:
            w_copy(11).start()
        if j == 2:
            stores[0].start()

    def level(which):
        if which == 1:
            for k in range(7):
                small_from(k).wait_recv()
            total = s_got[0]
            for g in range(1, 8):
                total = total + s_got[g]
            s_total[...] = total
            for k in range(3):
                level_to(k).start()
            s_all[p.z] = total
            for j in range(4):
                to_pair(j, gi, block_cols(j)).wait_send()
            to_pair(4, ga, whole).wait_send()
            for j in range(3):
                for half in range(2):
                    to_pair(5 + 3 * half + j, gq, pl.ds(j * 1024 + 512 * half, 512)).wait_send()
            return
        for k in range(3):
            level_from(k).wait_recv()
        s_out[...] = (s_all[0] + s_all[1]) + (s_all[2] + s_all[3])
        stores[1].start()
        for k in range(7):
            small_to(k).wait_send()
        for k in range(3):
            level_to(k).wait_send()
        stores[0].wait()
        stores[1].wait()

    work = {
        "start": start, "down": down, "g": inner_step, "h": hidden_step, "u": up_block, "norm": first_norm,
        "gm": grad_mixed, "o": out_block, "at": attention, "q": qkv_block, "small": small, "t": token_step,
        "level": level, "begin": red.begin, "second": red.second, "along": red.along, "inward": red.inward,
        "hand": red.hand_out, "pass": red.hand_on, "close": red.close,
    }
    for name, *which in PLAN:
        work[name](*which)


def backward_call(lengths, saved):
    wq, wo, wu, wd, qkv, slope = saved[:6]
    rows, width = qkv.shape[0], wo.shape[0]
    ff = wu.shape[1]
    anyspace = pl.BlockSpec(memory_space=pl.ANY)
    shape = jax.ShapeDtypeStruct
    dma = pltpu.SemaphoreType.DMA
    outs = [
        shape((rows, width), F32),
        shape((width // 8, 3 * width), BF16),
        shape((width // 8, width), BF16),
        shape((width // 8, ff), BF16),
        shape((ff // 8, width), BF16),
        shape((16, 128), F32),
    ]
    scratch = [
        pltpu.VMEM((2, 2 * rows, 512), BF16),
        pltpu.VMEM((2, 1024, 1024), BF16),
        pltpu.VMEM((2, rows, 1024), BF16),
        pltpu.VMEM((2 * rows, width), BF16),
        pltpu.VMEM((2 * rows, ff), BF16),
        pltpu.VMEM((2 * rows, 3 * width), BF16),
        pltpu.VMEM((rows, width), BF16),
        pltpu.VMEM((rows, width), F32),
        pltpu.VMEM((rows, width), F32),
        pltpu.VMEM((rows, 128), F32),
        pltpu.VMEM((16, width), F32),
        pltpu.VMEM((8, width), F32),
        pltpu.VMEM((4, width), F32),
        pltpu.VMEM((BLOCKS, 2, 2, 128, 1024), BF16),
        pltpu.VMEM((BLOCKS, 2, 64, 1024), BF16),
        pltpu.VMEM((BLOCKS, 2, 64, 1024), BF16),
        pltpu.VMEM((BLOCKS, 64, 1024), BF16),
        pltpu.VMEM((BLOCKS, 64, 1024), BF16),
        pltpu.VMEM((BLOCKS, 128, 1024), BF16),
        pltpu.VMEM((BLOCKS, 64, 1024), BF16),
        pltpu.VMEM((len(SHARED), 2, 2, 64, 1024), BF16),
        pltpu.VMEM((8, 16, 128), F32),
        pltpu.VMEM((8, 16, 128), F32),
        pltpu.VMEM((16, 128), F32),
        pltpu.VMEM((4, 16, 128), F32),
        pltpu.VMEM((16, 128), F32),
        dma((10, len(PIECES))),
        dma((10, len(PIECES))),
        dma((len(PIECES),)),
        dma((11,)),
        dma((11,)),
        dma((7,)),
        dma((7, 4)),
        dma((12,)),
        dma((4,)),
        dma((7,)),
        dma((7,)),
        dma((3,)),
        dma((3,)),
        dma((2,)),
        dma((len(SHARED), 2)),
        dma((len(SHARED), 2)),
    ]
    return pl.pallas_call(
        backward_kernel,
        out_shape=outs,
        in_specs=[pl.BlockSpec(memory_space=pltpu.SMEM)] + [anyspace] * len(saved),
        out_specs=[anyspace] * len(outs),
        scratch_shapes=scratch,
        name="backward",
        cost_estimate=pl.CostEstimate(flops=4 * 512 * 12582912, bytes_accessed=60 * MIB, transcendentals=4 * MIB),
        compiler_params=pltpu.CompilerParams(
            collective_id=1, has_side_effects=True, vmem_limit_bytes=60 * MIB
        ),
    )(lengths, *saved)


def finish_kernel(
    layer_in, token_in, q_in, o_in, u_in, d_in, small,
    layer_out, token_out, q_out, o_out, u_out, d_out, biases_out, up_bias_out, gains_out,
    q_low, o_low, u_low, d_low, layer_v, token_v, small_v, q, o, u, d, sem,
):
    sources = (d_in, u_in, q_in, o_in, token_in, layer_in, small)
    lows, wides = (d_low, u_low, q_low, o_low, token_v, layer_v, small_v), (d, u, q, o, token_v, layer_v)
    results = (d_out, u_out, q_out, o_out, token_out, layer_out)
    ins = [pltpu.make_async_copy(a, b, sem.at[i]) for i, (a, b) in enumerate(zip(sources, lows))]
    outs = [pltpu.make_async_copy(a, b, sem.at[7 + i]) for i, (a, b) in enumerate(zip(wides, results))]
    for c in ins:
        c.start()
    for a, b, c_in, c_out in zip(lows, wides, ins, outs):
        c_in.wait()
        if a is not b:
            b[...] = a[...].astype(F32)
        c_out.start()
    ins[-1].wait()
    biases_out[...] = small_v[0:6]
    gains_out[...] = small_v[6:8]
    for i in range(4):
        up_bias_out[i * 128 : (i + 1) * 128] = small_v[8 + i]
    for c in outs:
        c.wait()


def finish_call(layer_out, token_grad, weight_grads, small):
    anyspace = pl.BlockSpec(memory_space=pl.ANY)
    vmem = pl.BlockSpec(memory_space=pltpu.VMEM)
    shape = jax.ShapeDtypeStruct
    wide = [shape(g.shape, F32) for g in weight_grads]
    outs = [
        shape(layer_out.shape, BF16), shape(token_grad.shape, F32), *wide,
        shape((6, 128), F32), shape((512,), F32), shape((2, 128), F32),
    ]
    return pl.pallas_call(
        finish_kernel,
        out_shape=outs,
        in_specs=[anyspace] * 7,
        out_specs=[anyspace] * 6 + [vmem] * 3,
        scratch_shapes=[pltpu.VMEM(g.shape, BF16) for g in weight_grads]
        + [pltpu.VMEM(g.shape, g.dtype) for g in (layer_out, token_grad, small)]
        + [pltpu.VMEM(g.shape, F32) for g in weight_grads]
        + [pltpu.SemaphoreType.DMA((13,))],
        name="finish",
        compiler_params=pltpu.CompilerParams(vmem_limit_bytes=60 * MIB),
    )(layer_out, token_grad, *weight_grads, small)


def plane(
    tokens,
    lengths,
    cotangent,
    qkv_weight,
    out_weight,
    up_weight,
    down_weight,
    biases,
    up_bias,
    gains,
):
    small_in = pack_small(biases, up_bias, gains)
    layer_out, *saved = forward_call(
        tokens, lengths, cotangent, qkv_weight, out_weight, up_weight, down_weight, small_in
    )
    token_grad, *weight_grads, small = backward_call(lengths, saved)
    return tuple(finish_call(layer_out, token_grad, weight_grads, small))


def solution(mesh):
    step = plane if dict(mesh.shape) == {"fsdp": 8, "rep": 4} else portable
    both = ("fsdp", "rep")
    in_specs = (
        P(both, None),
        P(both),
        P(both, None),
        P("fsdp", None),
        P("fsdp", None),
        P("fsdp", None),
        P("fsdp", None),
        P(None, "fsdp"),
        P("fsdp"),
        P(None, "fsdp"),
    )
    out_specs = (
        P(both, None),
        P(both, None),
        P("fsdp", None),
        P("fsdp", None),
        P("fsdp", None),
        P("fsdp", None),
        P(None, "fsdp"),
        P("fsdp"),
        P(None, "fsdp"),
    )
    return jax.shard_map(
        step, mesh=mesh, in_specs=in_specs, out_specs=out_specs, check_vma=False
    )
```

profile of v0, /device:TPU:0, one launch (start us, length us, event | category | flops | bytes accessed | tf_op | source)
XLA Modules:
  0.0 216.9 jit_solution(17228677114050738749)
XLA Ops:
  0.7 0.1 pad.3.clone
  0.7 1.4 maximum_maximum_fusion.small
  2.1 88.4 %forward.1 = (bf16[512,1024]{1,0:T(8,128)(2,1)}, bf16[1024,3072]{1,0:T(8,128)(2,1)}, bf16[1024,1024]{1,0:T(8,128)(2,1)}, bf16[1024,4096]{1,0:T(8,128)(2,1)}, bf1...) custom-call(s32[2]{0:T(128)} %lengths.3, ...), custom_call_target="tpu_custom_call" | custom-call | flops 12884901888 | bytes 62914560 | tf_op jit(solution)/shard_map/forward/pallas_call | solution.py:606
  90.5 120.5 %backward.1 = (f32[512,1024]{1,0:T(8,128)}, bf16[128,3072]{1,0:T(8,128)(2,1)}, bf16[128,1024]{1,0:T(8,128)(2,1)}, bf16[128,4096]{1,0:T(8,128)(2,1)}, bf16[512,1024]{1,0:T(8,128)(2,1)}, /*index=5*/f32[16,128]{1,0:T(8,128)}) custom-call(s32[2]{0:T(128)} %lengths.3, bf16[1024,3072]{1,0:T(8,128)(2,1)} %get-tuple-element.33.wq, ...), custom_call_target="tpu_custom_call" | custom-call | flops 25769803776 | bytes 62914560 | tf_op jit(solution)/shard_map/backward/pallas_call | solution.py:1197
  211.0 5.7 %finish.1 = (bf16[512,1024]{1,0:T(8,128)(2,1)}, f32[512,1024]{1,0:T(8,128)}, f32[128,3072]{1,0:T(8,128)}, f32[128,1024]{1,0:T(8,128)}, f32[128,4096]{1,0:T(8,128...) custom-call(bf16[512,1024]{1,0:T(8,128)(2,1)} %get-tuple-element.32.layer_in, ...), custom_call_target="tpu_custom_call" | custom-call | tf_op jit(solution)/shard_map/finish/pallas_call | solution.py:1246
  (1 shorter events, 0.0 us)
where the time goes:
time: 220 us; the launch traced here: 217 us
  Pallas kernels  215 us (98%)
    pallas_call x1, Pallas kernels, backward_call(): pl.pallas_call(backward_kernel, out_shape=outs, in_specs=[pl.BlockSpec(me...  120 us
    pallas_call x1, Pallas kernels, forward_call(): pl.pallas_call(forward_kernel, out_shape=outs, in_specs=[pl.BlockSpec(mem...  88.4 us
    pallas_call x1, Pallas kernels, finish_call(): pl.pallas_call(finish_kernel, out_shape=outs, in_specs=[anyspace] * 7, ou...  5.71 us

commit v1 on v0

--- a/solution.py
+++ b/solution.py
@@ -322,12 +322,12 @@
 
 
 def forward_kernel(
-    lengths, tokens, cot, small, sh_q, sh_o, sh_u, sh_d,
+    lengths, biases, up_bias, gains, tokens, cot, sh_q, sh_o, sh_u, sh_d,
     layer_out, wq_out, wo_out, wu_out, wd_out, qkv_out, slope_out, act_pair, first_pair, mixed_pair,
     tok_pair, branch_pair, norm_out, inv_out, grad_out_ref, params_out, sums_out,
     x, wq, wo, wu, wd, qkv, mixed, norm, first_low, act, slope, acc, cot_v, gh2, out_v, gb, smalls, params,
-    inv_v, sums, up_rows,
-    ag_send, ag_recv, ag_local, sm_send, sm_recv, sm_local, io, pair_send, pair_recv, pair_local, wd_sem,
+    inv_v, sums, up_rows, small,
+    ag_send, ag_recv, ag_local, sm_send, sm_recv, io, pair_send, pair_recv, pair_local, wd_sem,
 ):
     p = Place()
     rows, width = x.shape
@@ -341,10 +341,15 @@
     loads = [
         pltpu.make_async_copy(tokens, x, io.at[0]),
         pltpu.make_async_copy(cot, cot_v, io.at[1]),
-        pltpu.make_async_copy(small, smalls.at[p.f], sm_local),
     ]
     for c in loads:
         c.start()
+    small[...] = jnp.zeros_like(small)
+    small[0:6] = biases[...].astype(F32)
+    small[6:8] = gains[...].astype(F32)
+    for i in range(4):
+        small[8 + i] = up_bias[i * 128 : (i + 1) * 128].astype(F32)
+    smalls[p.f] = small[...]
     pl.semaphore_wait(barrier, 8)
 
     def small_copy(k, owner, device):
@@ -384,12 +389,11 @@
     def small_params(_):
         loads[0].wait()
         start_pair(0, x, tok_pair, 128)
-        loads[2].wait()
         for k in range(7):
             back = lax.rem(p.f + 7 - k, 8)
             small_copy(k, back, p.dev(f=back)).wait_recv()
         for g in range(8):
-            part = smalls[g].astype(F32)
+            part = smalls[g]
             params[:, g * 128 : (g + 1) * 128] = part
             for j in range(4):
                 up_rows[g : g + 1, j * 128 : (j + 1) * 128] = part[8 + j : 9 + j]
@@ -544,7 +548,7 @@
         work[name](*which)
 
 
-def forward_call(tokens, lengths, cotangent, qkv_w, out_w, up_w, down_w, small):
+def forward_call(tokens, lengths, cotangent, qkv_w, out_w, up_w, down_w, biases, up_bias, gains):
     rows, width = tokens.shape
     ff = up_w.shape[1]
     anyspace = pl.BlockSpec(memory_space=pl.ANY)
@@ -586,17 +590,17 @@
         pltpu.VMEM((rows, width), F32),
         pltpu.VMEM((rows, width), BF16),
         pltpu.VMEM((rows, width), BF16),
-        pltpu.VMEM((8, 16, 128), BF16),
+        pltpu.VMEM((8, 16, 128), F32),
         pltpu.VMEM((16, width), F32),
         pltpu.VMEM((rows, 128), F32),
         pltpu.VMEM((8, width), F32),
         pltpu.VMEM((8, ff // 8), F32),
+        pltpu.VMEM((16, 128), F32),
         dma((len(UNITS), KINDS)),
         dma((len(UNITS), KINDS)),
         dma((len(UNITS),)),
         dma((7,)),
         dma((7,)),
-        dma,
         dma((14,)),
         dma((5, 4)),
         dma((5, 4)),
@@ -606,7 +610,7 @@
     return pl.pallas_call(
         forward_kernel,
         out_shape=outs,
-        in_specs=[pl.BlockSpec(memory_space=pltpu.SMEM)] + [anyspace] * 7,
+        in_specs=[pl.BlockSpec(memory_space=pltpu.SMEM)] + [pl.BlockSpec(memory_space=pltpu.VMEM)] * 3 + [anyspace] * 6,
         out_specs=[anyspace] * len(outs),
         scratch_shapes=scratch,
         name="forward",
@@ -614,24 +618,21 @@
         compiler_params=pltpu.CompilerParams(
             collective_id=0, has_side_effects=True, vmem_limit_bytes=60 * MIB
         ),
-    )(lengths, tokens, cotangent, small, qkv_w, out_w, up_w, down_w)
-
-
-def pack_small(biases, up_bias, gains):
-    return jnp.concatenate([biases, gains, up_bias.reshape(4, 128), jnp.zeros((4, 128), BF16)], axis=0)
+    )(lengths, biases, up_bias, gains, tokens, cotangent, qkv_w, out_w, up_w, down_w)
 
 
 BLOCKS = 12
-SHARED = (2, 3)
+FAR = 2
+SHARED = (1, 2)
 PIECES = (
     (0, 0, 64),
-    (1, 0, 64),
+    (3, 0, 64),
     (2, None, 32),
     (4, 0, 64),
-    (3, None, 32),
+    (1, None, 32),
     (5, 0, 64),
+    (7, 0, 64),
     (6, 0, 64),
-    (7, 0, 64),
     (8, 0, 64),
     (9, 0, 32),
     (9, 32, 32),
@@ -643,28 +644,28 @@
     (11, 48, 16),
 )
 PLAN = (
-    ("start", 0), ("down", 0), ("begin", 0), ("down", 1), ("begin", 1), ("down", 2), ("down", 3), ("g", 0),
-    ("h", 0), ("second", 0), ("g", 1), ("h", 1), ("u", 0), ("second", 1), ("begin", 3), ("g", 2),
-    ("along", 0), ("h", 2), ("u", 1), ("along", 1), ("begin", 2), ("g", 3), ("begin", 5), ("h", 3), ("u", 2),
-    ("second", 3), ("norm", 0), ("second", 2), ("u", 3), ("inward", 0), ("begin", 4), ("gm", 0),
-    ("second", 5), ("o", 0), ("at", 0, 1), ("hand", 0), ("inward", 1), ("along", 3), ("at", 1, 2),
-    ("along", 2), ("begin", 6), ("at", 2, 4), ("second", 4), ("at", 4, 5), ("pass", 0), ("inward", 3),
-    ("at", 5, 6), ("along", 5), ("at", 6, 7), ("hand", 1), ("begin", 7), ("inward", 2), ("at", 7, 8),
-    ("at", 8, 9), ("hand", 3), ("at", 9, 10), ("inward", 5), ("pass", 1), ("second", 6), ("at", 10, 11),
-    ("along", 4), ("at", 11, 12), ("hand", 2), ("at", 12, 13), ("inward", 4), ("begin", 8), ("at", 13, 14),
-    ("pass", 3), ("at", 14, 15), ("second", 7), ("at", 15, 16), ("hand", 5), ("q", 0), ("along", 6), ("q", 1),
-    ("close", 0), ("pass", 2), ("begin", 9), ("q", 2), ("hand", 4), ("inward", 6), ("small", 0),
-    ("second", 8), ("pass", 5), ("t", 0), ("t", 1), ("pass", 4), ("along", 7), ("begin", 10), ("close", 1),
-    ("t", 2), ("second", 9), ("hand", 6), ("level", 1), ("inward", 7), ("begin", 11), ("along", 8),
-    ("begin", 12), ("second", 10), ("along", 9), ("close", 3), ("begin", 13), ("pass", 6), ("inward", 8),
-    ("begin", 14), ("hand", 7), ("inward", 9), ("hand", 8), ("second", 11), ("close", 2), ("begin", 15),
-    ("pass", 7), ("hand", 9), ("second", 12), ("along", 10), ("inward", 10), ("begin", 16), ("close", 5),
-    ("second", 13), ("second", 14), ("along", 11), ("close", 4), ("second", 15), ("pass", 8), ("inward", 11),
-    ("pass", 9), ("along", 12), ("second", 16), ("hand", 10), ("along", 13), ("inward", 12), ("along", 14),
-    ("hand", 11), ("along", 15), ("along", 16), ("inward", 13), ("close", 6), ("pass", 10), ("inward", 14),
-    ("hand", 12), ("inward", 15), ("pass", 11), ("inward", 16), ("hand", 13), ("hand", 14), ("close", 7),
-    ("pass", 12), ("hand", 15), ("level", 2), ("hand", 16), ("pass", 13), ("pass", 14), ("pass", 15),
-    ("pass", 16), ("close", 8), ("close", 9), ("close", 10), ("close", 11), ("close", 12), ("close", 13),
+    ("start", 0), ("down", 0), ("begin", 0), ("down", 1), ("swap", 1, 0), ("swap", 1, 1), ("down", 2),
+    ("down", 3), ("swap", 2, 0), ("begin", 1), ("g", 0), ("h", 0), ("second", 0), ("g", 1), ("swap", 2, 1),
+    ("h", 1), ("second", 1), ("u", 0), ("begin", 4), ("along", 0), ("begin", 3), ("g", 2), ("along", 1),
+    ("h", 2), ("u", 1), ("second", 4), ("begin", 5), ("g", 3), ("h", 3), ("u", 2), ("second", 3),
+    ("along", 4), ("inward", 0), ("norm", 0), ("begin", 2), ("u", 3), ("second", 5), ("hand", 0),
+    ("inward", 1), ("gm", 0), ("begin", 6), ("o", 0), ("along", 3), ("inward", 4), ("at", 0, 1),
+    ("second", 2), ("pass", 0), ("at", 1, 3), ("hand", 1), ("inward", 3), ("along", 5), ("at", 3, 4),
+    ("begin", 7), ("at", 4, 5), ("hand", 4), ("at", 5, 7), ("second", 6), ("pass", 1), ("inward", 5),
+    ("at", 7, 8), ("along", 2), ("hand", 3), ("at", 8, 10), ("inward", 2), ("pass", 4), ("begin", 8),
+    ("at", 10, 12), ("second", 7), ("hand", 5), ("at", 12, 14), ("pass", 3), ("along", 6), ("close", 0),
+    ("at", 14, 16), ("hand", 2), ("q", 0), ("inward", 6), ("begin", 9), ("pass", 5), ("q", 1), ("second", 8),
+    ("q", 2), ("pass", 2), ("along", 7), ("begin", 10), ("close", 1), ("small", 0), ("hand", 6),
+    ("begin", 11), ("t", 0), ("second", 9), ("inward", 7), ("t", 1), ("along", 8), ("close", 4), ("t", 2),
+    ("pass", 6), ("begin", 12), ("level", 1), ("inward", 8), ("second", 10), ("hand", 7), ("begin", 13),
+    ("close", 3), ("second", 11), ("along", 9), ("begin", 14), ("begin", 15), ("second", 12), ("hand", 8),
+    ("inward", 9), ("along", 10), ("close", 5), ("begin", 16), ("second", 13), ("pass", 7), ("along", 11),
+    ("close", 2), ("inward", 10), ("pass", 8), ("second", 14), ("hand", 9), ("inward", 11), ("hand", 10),
+    ("second", 15), ("along", 12), ("second", 16), ("along", 13), ("along", 14), ("pass", 9), ("close", 6),
+    ("inward", 12), ("hand", 11), ("along", 15), ("along", 16), ("pass", 10), ("inward", 13), ("inward", 14),
+    ("hand", 12), ("inward", 15), ("pass", 11), ("hand", 13), ("hand", 14), ("inward", 16), ("pass", 12),
+    ("hand", 15), ("level", 2), ("pass", 13), ("close", 7), ("pass", 14), ("hand", 16), ("pass", 15),
+    ("close", 8), ("pass", 16), ("close", 9), ("close", 10), ("close", 11), ("close", 12), ("close", 13),
     ("close", 14), ("close", 15), ("close", 16),
 )
 S1X, S1Y, S2X, S2Y, Z1G, Z1K, Z2, FM, FE, FF = range(10)
@@ -726,6 +727,8 @@
             src, dst, dev = own.at[keep], self.out_at(b, keep if sending else give), to_other
         elif kind == FE:
             src, dst, dev = own.at[keep], self.out_at(b, keep), to_end
+        elif u >= len(PIECES) - FAR:
+            src, dst, dev = own.at[keep], self.out_at(b, keep if sending else give), p.dev(z=3 - self.end)
         else:
             src, dst, dev = self.out_at(b, give), self.out_at(b, give), to_end
         return remote(src, dst, self.send.at[kind, u], self.recv.at[kind, u], dev)
@@ -736,10 +739,8 @@
         dst = self.swapped.at[i, :, :, pl.ds(32 * half, 32)]
         return remote(src, dst, self.swap_send.at[i, half], self.swap_recv.at[i, half], self.p.dev(z=self.p.zn))
 
-    def produced(self, b):
-        if b in SHARED:
-            self.swap(b, 0).start()
-            self.swap(b, 1).start()
+    def swap_out(self, b, half):
+        self.swap(b, half).start()
 
     def begin(self, u):
         b, o, n = self.rows(u)
@@ -813,6 +814,8 @@
             if b not in SHARED:
                 total = total + self.from_end[b, keep].astype(F32)
             self.prod[b, y, x, keep] = total.astype(BF16)
+            if u >= len(PIECES) - FAR:
+                self.copy(FF, u).start()
             self.copy(FM, u).start()
             self.copy(FE, u).start()
             self.write(u).start()
@@ -821,7 +824,8 @@
         @pl.when(self.is_mid)
         def _():
             self.copy(FM, u, False).wait_recv()
-            self.copy(FF, u).start()
+            if u < len(PIECES) - FAR:
+                self.copy(FF, u).start()
 
     def close(self, u):
         for kind in (S1X, S1Y, S2X, S2Y):
@@ -903,12 +907,6 @@
     for c in lhs_copies(0):
         c.start()
     loads[0].start()
-    for c in lhs_copies(1):
-        c.start()
-    w_copy(0).start()
-    slope_copy(0).start()
-    for c in loads[1:]:
-        c.start()
 
     def out_at(b, at):
         if b < 4:
@@ -926,7 +924,6 @@
 
     def produce(b, left, right):
         prod[b] = dot_tn(left, right).astype(BF16).reshape(2, 2, 128, 1024)
-        red.produced(b)
 
     def to_pair(index, ref, cols):
         here = ref.at[mine, cols]
@@ -939,15 +936,24 @@
     ga = branch
 
     def start(_):
-        pl.semaphore_wait(barrier, 10)
+        for c in lhs_copies(0):
+            c.wait()
         loads[0].wait()
+        for c in lhs_copies(1):
+            c.start()
+        w_copy(0).start()
+        slope_copy(0).start()
+        for c in loads[1:]:
+            c.start()
 
     def down(b):
-        for c in lhs_copies(b):
+        for c in lhs_copies(b) if b > 0 else ():
             c.wait()
         produce(b, lhs[b % 2], branch[...])
         for c in lhs_copies(b + 2):
             c.start()
+        if b == 0:
+            pl.semaphore_wait(barrier, 10)
         if b == 3:
             loads[1].wait()
 
@@ -1129,7 +1135,7 @@
         "start": start, "down": down, "g": inner_step, "h": hidden_step, "u": up_block, "norm": first_norm,
         "gm": grad_mixed, "o": out_block, "at": attention, "q": qkv_block, "small": small, "t": token_step,
         "level": level, "begin": red.begin, "second": red.second, "along": red.along, "inward": red.inward,
-        "hand": red.hand_out, "pass": red.hand_on, "close": red.close,
+        "swap": red.swap_out, "hand": red.hand_out, "pass": red.hand_on, "close": red.close,
     }
     for name, *which in PLAN:
         work[name](*which)
@@ -1269,9 +1275,8 @@
     up_bias,
     gains,
 ):
-    small_in = pack_small(biases, up_bias, gains)
     layer_out, *saved = forward_call(
-        tokens, lengths, cotangent, qkv_weight, out_weight, up_weight, down_weight, small_in
+        tokens, lengths, cotangent, qkv_weight, out_weight, up_weight, down_weight, biases, up_bias, gains
     )
     token_grad, *weight_grads, small = backward_call(lengths, saved)
     return tuple(finish_call(layer_out, token_grad, weight_grads, small))

time: 220 us -> 219 us (level)
  no operation moved by 1% of the time
where the time goes in v1:
time: 219 us; the launch traced here: 215 us
  Pallas kernels  214 us (98%)
    pallas_call x1, Pallas kernels, backward_call(): pl.pallas_call(backward_kernel, out_shape=outs, in_specs=[pl.BlockSpec(me...  120 us
    pallas_call x1, Pallas kernels, forward_call(): pl.pallas_call(forward_kernel, out_shape=outs, in_specs=[pl.BlockSpec(mem...  88.7 us
    pallas_call x1, Pallas kernels, finish_call(): pl.pallas_call(finish_kernel, out_shape=outs, in_specs=[anyspace] * 7, ou...  5.71 us

profile of v1, /device:TPU:0, one launch (start us, length us, event | category | flops | bytes accessed | tf_op | source)
XLA Modules:
  0.0 215.2 jit_solution(7625320865720381907)
XLA Ops:
  0.6 88.7 %forward.1 = (bf16[512,1024]{1,0:T(8,128)(2,1)}, bf16[1024,3072]{1,0:T(8,128)(2,1)}, bf16[1024,1024]{1,0:T(8,128)(2,1)}, bf16[1024,4096]{1,0:T(8,128)(2,1)}, bf1...) custom-call(s32[2]{0:T(128)} %lengths.3, ...), custom_call_target="tpu_custom_call" | custom-call | flops 12884901888 | bytes 62914560 | tf_op jit(solution)/shard_map/forward/pallas_call | solution.py:610
  89.4 119.6 %backward.1 = (f32[512,1024]{1,0:T(8,128)}, bf16[128,3072]{1,0:T(8,128)(2,1)}, bf16[128,1024]{1,0:T(8,128)(2,1)}, bf16[128,4096]{1,0:T(8,128)(2,1)}, bf16[512,1024]{1,0:T(8,128)(2,1)}, /*index=5*/f32[16,128]{1,0:T(8,128)}) custom-call(s32[2]{0:T(128)} %lengths.3, bf16[1024,3072]{1,0:T(8,128)(2,1)} %get-tuple-element.33.wq, ...), custom_call_target="tpu_custom_call" | custom-call | flops 25769803776 | bytes 62914560 | tf_op jit(solution)/shard_map/backward/pallas_call | solution.py:1203
  209.0 5.7 %finish.1 = (bf16[512,1024]{1,0:T(8,128)(2,1)}, f32[512,1024]{1,0:T(8,128)}, f32[128,3072]{1,0:T(8,128)}, f32[128,1024]{1,0:T(8,128)}, f32[128,4096]{1,0:T(8,128...) custom-call(bf16[512,1024]{1,0:T(8,128)(2,1)} %get-tuple-element.32.layer_in, ...), custom_call_target="tpu_custom_call" | custom-call | tf_op jit(solution)/shard_map/finish/pallas_call | solution.py:1252

commit v2 on v1

--- a/solution.py
+++ b/solution.py
@@ -327,7 +327,7 @@
     tok_pair, branch_pair, norm_out, inv_out, grad_out_ref, params_out, sums_out,
     x, wq, wo, wu, wd, qkv, mixed, norm, first_low, act, slope, acc, cot_v, gh2, out_v, gb, smalls, params,
     inv_v, sums, up_rows, small,
-    ag_send, ag_recv, ag_local, sm_send, sm_recv, io, pair_send, pair_recv, pair_local, wd_sem,
+    ag_send, ag_recv, ag_local, sm_send, sm_recv, io, pair_send, pair_recv, pair_local, wd_sem, half_sem,
 ):
     p = Place()
     rows, width = x.shape
@@ -500,30 +500,33 @@
 
     def second_norm(_):
         loads[1].wait()
-        hidden = acc[...]
-        center = hidden - row_mean(hidden)
-        inverse = lax.rsqrt(row_mean(center * center) + 1e-05)
-        second = center * inverse
-        row_at = lax.broadcasted_iota(jnp.int32, (seq, 1), 0)
-        live = jnp.concatenate([(row_at < lengths[s]).astype(F32) for s in range(slots)], axis=0)
-        e = cot_v[...] * live
-        scaled = e * params[7:8]
-        gh2[...] = inverse * (scaled - row_mean(scaled) - second * row_mean(scaled * second))
-        gb[...] = gh2[...].astype(BF16)
-        swap = (
-            pltpu.make_async_copy(gb, branch_pair.at[mine], pair_local.at[4, 0]),
-            remote(gb, branch_pair.at[mine], pair_send.at[4, 0], pair_recv.at[4, 0], p.dev(f=p.fs)),
-        )
-        for c in swap:
-            c.start()
-        store(gh2, grad_out_ref, io.at[11])
+        swap = []
+        totals = []
+        for s in range(slots):
+            at = pl.ds(s * seq, seq)
+            hidden = acc[at]
+            center = hidden - row_mean(hidden)
+            inverse = lax.rsqrt(row_mean(center * center) + 1e-05)
+            second = center * inverse
+            row_at = lax.broadcasted_iota(jnp.int32, (seq, 1), 0)
+            e = cot_v[at] * (row_at < lengths[s]).astype(F32)
+            scaled = e * params[7:8]
+            gh2[at] = inverse * (scaled - row_mean(scaled) - second * row_mean(scaled * second))
+            gb[at] = gh2[at].astype(BF16)
+            src = gb.at[at]
+            dst = branch_pair.at[pl.ds(pl.multiple_of(p.core * rows + s * seq, seq), seq)]
+            swap.append(remote(src, dst, pair_send.at[4, s], pair_recv.at[4, s], p.dev(f=p.fs)))
+            swap.append(pltpu.make_async_copy(src, dst, pair_local.at[4, s]))
+            for c in swap[-2:]:
+                c.start()
+            store(gh2.at[at], grad_out_ref.at[at], half_sem.at[0, s])
+            out_v[at] = (second * params[7:8] + params[5:6]).astype(BF16)
+            store(out_v.at[at], layer_out.at[at], half_sem.at[1, s])
+            totals.append([jnp.sum(t, axis=0, keepdims=True) for t in (e * second, e, gb[at].astype(F32))])
         store(params, params_out, io.at[12])
-        out_v[...] = (second * params[7:8] + params[5:6]).astype(BF16)
-        store(out_v, layer_out, io.at[10])
         sums[...] = jnp.zeros_like(sums)
-        sums[0:1] = jnp.sum(e * second, axis=0, keepdims=True)
-        sums[1:2] = jnp.sum(e, axis=0, keepdims=True)
-        sums[2:3] = jnp.sum(gb[...].astype(F32), axis=0, keepdims=True)
+        for i in range(3):
+            sums[i : i + 1] = sum(t[i] for t in totals)
         store(sums, sums_out, io.at[13])
         for part in parts:
             if UNITS[part.unit][0] == "d":
@@ -606,6 +609,7 @@
         dma((5, 4)),
         dma((5, 4)),
         dma((8, len(UNITS))),
+        dma((2, 2)),
     ]
     return pl.pallas_call(
         forward_kernel,

time: 219 us -> 218 us (level)
  no operation moved by 1% of the time
where the time goes in v2:
time: 218 us; the launch traced here: 215 us
  Pallas kernels  214 us (98%)
    pallas_call x1, Pallas kernels, backward_call(): pl.pallas_call(backward_kernel, out_shape=outs, in_specs=[pl.BlockSpec(me...  120 us
    pallas_call x1, Pallas kernels, forward_call(): pl.pallas_call(forward_kernel, out_shape=outs, in_specs=[pl.BlockSpec(mem...  88.2 us
    pallas_call x1, Pallas kernels, finish_call(): pl.pallas_call(finish_kernel, out_shape=outs, in_specs=[anyspace] * 7, ou...  5.71 us

profile of v2, /device:TPU:0, one launch (start us, length us, event | category | flops | bytes accessed | tf_op | source)
XLA Modules:
  0.0 214.7 jit_solution(14182939487492636529)
XLA Ops:
  0.6 88.2 %forward.1 = (bf16[512,1024]{1,0:T(8,128)(2,1)}, bf16[1024,3072]{1,0:T(8,128)(2,1)}, bf16[1024,1024]{1,0:T(8,128)(2,1)}, bf16[1024,4096]{1,0:T(8,128)(2,1)}, bf1...) custom-call(s32[2]{0:T(128)} %lengths.3, ...), custom_call_target="tpu_custom_call" | custom-call | flops 12884901888 | bytes 62914560 | tf_op jit(solution)/shard_map/forward/pallas_call | solution.py:614
  88.8 119.6 %backward.1 = (f32[512,1024]{1,0:T(8,128)}, bf16[128,3072]{1,0:T(8,128)(2,1)}, bf16[128,1024]{1,0:T(8,128)(2,1)}, bf16[128,4096]{1,0:T(8,128)(2,1)}, bf16[512,1024]{1,0:T(8,128)(2,1)}, /*index=5*/f32[16,128]{1,0:T(8,128)}) custom-call(s32[2]{0:T(128)} %lengths.3, bf16[1024,3072]{1,0:T(8,128)(2,1)} %get-tuple-element.33.wq, ...), custom_call_target="tpu_custom_call" | custom-call | flops 25769803776 | bytes 62914560 | tf_op jit(solution)/shard_map/backward/pallas_call | solution.py:1207
  208.5 5.7 %finish.1 = (bf16[512,1024]{1,0:T(8,128)(2,1)}, f32[512,1024]{1,0:T(8,128)}, f32[128,3072]{1,0:T(8,128)}, f32[128,1024]{1,0:T(8,128)}, f32[128,4096]{1,0:T(8,128...) custom-call(bf16[512,1024]{1,0:T(8,128)(2,1)} %get-tuple-element.32.layer_in, ...), custom_call_target="tpu_custom_call" | custom-call | tf_op jit(solution)/shard_map/finish/pallas_call | solution.py:1256
